TPU v7x, 128 devices: a whole 4x4x4 slice. The times are simulated.
128 devices in a mesh: tiles: 128 (over z, x, y, core).
Axes of the slice: x: 4, y: 4, z: 4, core: 2. Of those that a mesh axis runs over, the one named last changes fastest.
Arguments:
- prognostic: float32 [128, 2, 384, 450], P('tiles'), may hold values from -6 to 6
- cutoffs: int32 [32], replicated, may hold values from 24 to 191, as said below
- listed: int32 [128, 5], P('tiles'), may hold values from -1 to 5, as said below
- weight_in: bfloat16 [384, 512], replicated, may hold values from -0.3125 to 0.3125
- weight_mid: bfloat16 [512, 512], replicated, may hold values from -0.25 to 0.25
- weight_out: bfloat16 [512, 384], replicated, may hold values from -0.25 to 0.25
Outputs:
- updated: float32 [128, 2, 384, 450], P('tiles')
Inputs may be any that keep to these rules, and one draw needn't show every extreme that they name: `cutoffs`: Non-increasing along the rows; the first row holds the largest value and the last row the smallest. `listed`: row t names distinct blocks first and -1 after them; row t and row t XOR (64) name exactly 6 blocks together; some row names 5 blocks.
All inputs are finite; a program needn't handle non-finite values.
Results may differ from a plain program's by a relative error of at most 0.00094.
Values may be sent and summed in bfloat16 or wider, within the bound.
A program may use at most 192 MiB of HBM per device.

v0:
```python
import math

import jax
import jax.numpy as jnp
from jax import lax
from jax.sharding import PartitionSpec as P

NLON = 3600
KMAX = 192


def physics_net(columns, weight_in, weight_mid, weight_out):
    first = jnp.einsum("ch,scb->shb", weight_in, columns, preferred_element_type=jnp.float32)
    first = jax.nn.silu(first).astype(jnp.bfloat16)
    second = jnp.einsum("hg,shb->sgb", weight_mid, first, preferred_element_type=jnp.float32)
    second = jax.nn.silu(second).astype(jnp.bfloat16)
    return jnp.einsum("gc,sgb->scb", weight_out, second, preferred_element_type=jnp.float32)


def local(prognostic, cutoffs, listed, weight_in, weight_mid, weight_out):
    devices = lax.axis_size("tiles")
    device_id = lax.axis_index("tiles")
    rows_here = prognostic.shape[1]
    channels = prognostic.shape[2]
    segment = prognostic.shape[3]
    lat_count = devices // 8
    units_piece = rows_here * channels // devices
    unit_ids = device_id * units_piece + jnp.arange(units_piece, dtype=jnp.int32)
    row_ids = (
        jnp.arange(lat_count, dtype=jnp.int32)[None, :] * rows_here
        + (unit_ids // channels)[:, None]
    )
    limits = jnp.take(cutoffs, row_ids.reshape(-1), axis=0)
    points = jnp.arange(NLON, dtype=jnp.int32)
    numbers = jnp.arange(KMAX, dtype=jnp.int32)
    radians = (points[:, None] * numbers[None, :] % NLON).astype(jnp.float32) * (
        2.0 * math.pi / NLON
    )
    cosine = jnp.cos(radians)
    sine = jnp.sin(radians)
    factors = jnp.where(numbers == 0, 1.0, 2.0).astype(jnp.float32) / NLON
    scaling = jnp.where(numbers[None, :] <= limits[:, None], factors[None, :], 0.0)
    pieces = prognostic.reshape(devices, units_piece, segment)
    circles = lax.all_to_all(pieces, "tiles", split_axis=0, concat_axis=2, tiled=True)
    circles = circles.reshape(units_piece, 8, lat_count, segment).transpose(0, 2, 1, 3)
    circles = circles.reshape(units_piece * lat_count, NLON)
    coef_cos = (
        jnp.dot(
            circles, cosine, precision=lax.Precision.HIGHEST, preferred_element_type=jnp.float32
        )
        * scaling
    )
    coef_sin = (
        jnp.dot(circles, sine, precision=lax.Precision.HIGHEST, preferred_element_type=jnp.float32)
        * scaling
    )
    smooth = jnp.dot(
        coef_cos, cosine.T, precision=lax.Precision.HIGHEST, preferred_element_type=jnp.float32
    ) + jnp.dot(
        coef_sin, sine.T, precision=lax.Precision.HIGHEST, preferred_element_type=jnp.float32
    )
    smooth = smooth.reshape(units_piece, lat_count, 8, segment).transpose(0, 2, 1, 3)
    smooth = smooth.reshape(1, units_piece, devices * segment)
    homed = lax.all_to_all(smooth, "tiles", split_axis=2, concat_axis=0, tiled=True)
    filtered = homed.reshape(rows_here, channels, segment)
    block_lon = segment // 3
    blocks_dev = 3 * rows_here
    blocks = filtered.reshape(rows_here, channels, 3, block_lon).transpose(0, 2, 1, 3)
    blocks = blocks.reshape(blocks_dev, channels, block_lon)
    block_list = listed[0]
    picked = jnp.take(blocks, jnp.clip(block_list, 0, blocks_dev - 1), axis=0).astype(jnp.bfloat16)
    tendency = physics_net(picked, weight_in, weight_mid, weight_out)
    target = jnp.where(block_list >= 0, block_list, blocks_dev)
    result = blocks.at[target].add(tendency, mode="drop")
    result = result.reshape(rows_here, 3, channels, block_lon).transpose(0, 2, 1, 3)
    return result.reshape(1, rows_here, channels, segment)


def solution(mesh):
    return jax.shard_map(
        local,
        mesh=mesh,
        in_specs=(P("tiles", None, None, None), P(), P("tiles", None), P(), P(), P()),
        out_specs=P("tiles", None, None, None),
        check_vma=False,
    )
```

profile of v0, /device:TPU:0, one launch (start us, length us, event | category | flops | bytes accessed | tf_op | source)
XLA Modules:
  0.0 564.6 jit_solution(12227584958652276688)
XLA Ops:
  0.0 2.5 copy.14
  2.5 1.6 reshape.156
  4.1 11.1 %all-to-all-start = ((f32[128,6,450]{2,1,0:T(8,128)}), f32[128,6,450]{2,1,0:T(8,128)S(1)}, u32[]{:S(2)}, u32[]{:S(2)}) async-start(f32[128,6,450]{2,1,0:T(8,128)} %reshape.156), calls=%async_computation | async-start | bytes 4194304 | tf_op jit(solution)/shard_map/all_to_all | solution.py:44
  15.6 1.2 gather_fusion
  16.8 28.8 %all-to-all-done = f32[128,6,450]{2,1,0:T(8,128)S(1)} async-done(((f32[128,6,450]{2,1,0:T(8,128)}), f32[128,6,450]{2,1,0:T(8,128)S(1)}, u32[]{:S(2)}, u32[]{:S(2)}) %all-to-all-start) | async-done | bytes 1382432 | tf_op jit(solution)/shard_map/all_to_all | solution.py:44
  45.6 2.1 copy.26
  47.7 2.7 reshape.158
  50.4 19.8 %fusion.40 = f32[96,192]{0,1:T(8,128)S(1)} fusion(f32[96,3600]{1,0:T(8,128)S(1)} %reshape.158, f32[192]{0:T(256)S(1)} %fusion.53, s32[96]{0:T(128)S(1)} %and_select_fusion), kind=kOutput, calls=%fused_computation.42 | convolution fusion | flops 802538496 | bytes 1457280 | tf_op jit(solution)/shard_map/dot_general | solution.py:48
  70.2 20.3 %fusion.43 = f32[96,192]{0,1:T(8,128)S(1)} fusion(f32[96,3600]{1,0:T(8,128)S(1)} %reshape.158, f32[192]{0:T(256)S(1)} %fusion.53, s32[96]{0:T(128)S(1)} %and_select_fusion), kind=kOutput, calls=%fused_computation.43 | convolution fusion | flops 802538496 | bytes 1457280 | tf_op jit(solution)/shard_map/dot_general | solution.py:54
  90.5 17.6 %fusion.6 = f32[96,3600]{1,0:T(8,128)S(1)} fusion(f32[96,192]{0,1:T(8,128)S(1)} %fusion.40), kind=kOutput, calls=%fused_computation.12 | convolution fusion | flops 802483200 | bytes 1456128 | tf_op jit(solution)/shard_map/dot_general | solution.py:57
  108.0 18.1 %convolution_add_fusion = f32[96,3600]{1,0:T(8,128)S(1)} fusion(f32[96,3600]{1,0:T(8,128)S(1)} %fusion.6, f32[96,192]{0,1:T(8,128)S(1)} %fusion.43), kind=kOutput, calls=%fused_computation.4 | convolution fusion | flops 802828800 | bytes 2838528 | tf_op jit(solution)/shard_map/dot_general | solution.py:59
  126.2 1.5 reshape.159
  127.7 2.1 copy.25
  129.8 2.7 reshape.160
  132.4 41.2 %copy.17 = f32[1,6,57600]{1,0,2:T(1,128)} copy(f32[1,6,57600]{2,1,0:T(8,128)S(1)} %reshape.160) | data formatting | bytes 2764800 | tf_op jit(solution)/shard_map/reshape | solution.py:63
  173.7 0.5 broadcast.211
  174.2 268.4 %reduce.1 = f32[57600,6]{1,0:T(8,128)} reduce(f32[57600,1,6]{2,1,0:T(1,128)} %bitcast.95, f32[]{:T(128)} %broadcast.211), dimensions={1}, to_apply=%bitcast.86.reduce_sub_computation | reduce | bytes 2764804
  442.5 21.2 %reshape.193 = f32[128,1,2700]{2,1,0:T(1,128)} reshape(f32[57600,6]{1,0:T(8,128)} %reduce.1) | data formatting | bytes 2764800
  463.7 4.8 all-to-all-start.1
  468.6 23.3 %all-to-all-done.1 = f32[128,1,2700]{2,1,0:T(1,128)S(1)} async-done(((f32[128,1,2700]{2,1,0:T(1,128)}), f32[128,1,2700]{2,1,0:T(1,128)S(1)}, u32[]{:S(2)}, u32[]{:S(2)}) %all-to-all-start.1) | async-done | bytes 1382432 | tf_op jit(solution)/shard_map/all_to_all | solution.py:64
  491.9 4.1 reduce.2
  496.0 33.8 %reshape.194 = f32[57600,1,6]{2,1,0:T(1,128)} reshape(f32[128,2700]{1,0:T(8,128)S(1)} %reduce.2) | data formatting | bytes 2764800
  529.8 15.2 %copy.22 = f32[6,57600]{1,0:T(8,128)S(1)} copy(f32[6,57600]{0,1:T(8,128)} %bitcast.96) | data formatting | bytes 2764800
  545.0 2.5 all_to_all.26
  547.5 2.4 copy.19
  549.9 3.2 reshape_reshape.3
  553.1 3.3 copy.20
  556.4 0.7 gather_fusion.1
  557.1 1.7 fusion.32
  558.8 2.4 convolution_bitcast_fusion
  561.2 1.3 scatter_fusion
  562.5 1.8 copy.21
  (20 shorter events, 0.3 us)
Async XLA Ops:
  0.0 558.8 %copy-start = (bf16[512,512]{1,0:T(8,128)(2,1)S(1)}, bf16[512,512]{1,0:T(8,128)(2,1)}, u32[]{:S(2)}) copy-start(bf16[512,512]{1,0:T(8,128)(2,1)} %param.10) | copy-start | bytes 1572868
  2.5 13.0 %copy-start.1 = (s32[32]{0:T(128)S(1)}, s32[32]{0:T(128)}, u32[]{:S(2)}) copy-start(s32[32]{0:T(128)} %param.7) | copy-start | bytes 388
  4.1 41.5 %all-to-all-start = ((f32[128,6,450]{2,1,0:T(8,128)}), f32[128,6,450]{2,1,0:T(8,128)S(1)}, u32[]{:S(2)}, u32[]{:S(2)}) async-start(f32[128,6,450]{2,1,0:T(8,128)} %reshape.156), calls=%async_computation | async-start | bytes 4194304 | tf_op jit(solution)/shard_map/all_to_all | solution.py:44
  442.5 26.1 %copy-start.3 = (s32[1,5]{1,0:T(1,128)S(1)}, s32[1,5]{1,0:T(1,128)}, u32[]{:S(2)}) copy-start(s32[1,5]{1,0:T(1,128)} %param.8) | copy-start | bytes 64
  463.7 28.2 %all-to-all-start.1 = ((f32[128,1,2700]{2,1,0:T(1,128)}), f32[128,1,2700]{2,1,0:T(1,128)S(1)}, u32[]{:S(2)}, u32[]{:S(2)}) async-start(f32[128,1,2700]{2,1,0:T(1,128)} %reshape.193), calls=%async_computation.1 | async-start | bytes 2883584 | tf_op jit(solution)/shard_map/all_to_all | solution.py:64
  553.1 4.0 copy-start.2
where the time goes:
time: 569 us; the launch traced here: 565 us
  other arithmetic  274 us (48%)
  local copies, waits for them, and re-layouts  142 us (25%)
  matrix products  79.8 us (14%)
  waiting for transfers between devices  52.1 us (9%)
  starting transfers between devices  16 us (3%)
    unnamed x1, other arithmetic  268 us
    unnamed x13, local copies, waits for them, and re-layouts  73.3 us
    reshape x2, local copies, waits for them, and re-layouts, local(): smooth = smooth.reshape(1, units_piece, devices * segment)  43.9 us
    all_to_all x1, waiting for transfers between devices, local(): lax.all_to_all(pieces, 'tiles', split_axis=0, concat_axis=2, tiled=True)  28.8 us
    all_to_all x1, waiting for transfers between devices, local(): lax.all_to_all(smooth, 'tiles', split_axis=2, concat_axis=0, tiled=True)  23.3 us
    dot_general x1, matrix products, local(): jnp.dot(circles, sine, precision=lax.Precision.HIGHEST, preferred_element...  20.3 us
    dot_general x1, matrix products, local(): jnp.dot(circles, cosine, precision=lax.Precision.HIGHEST, preferred_eleme...  19.8 us
    dot_general x1, matrix products, local(): jnp.dot(coef_sin, sine.T, precision=lax.Precision.HIGHEST, preferred_elem...  18.1 us
  transfers between devices with their start and end apart: 2, of which 2 were waited for; matrix products, arithmetic and copies ran while one was open for 0% of the time, Pallas kernels for 0%

commit v1 on v0

v1 whole, which is shorter than its diff:
```python
import math

import jax
import jax.numpy as jnp
import ml_dtypes
import numpy as np
from jax import lax
from jax.experimental import pallas as pl
from jax.experimental.pallas import tpu as pltpu
from jax.sharding import PartitionSpec as P

NLON = 3600
KMAX = 192
SEGMENTS = 8
SEG = NLON // SEGMENTS
COEFS = 2 * KMAX
LATS = 16
ROWS = 2
CHANNELS = 384
OWNED = CHANNELS // SEGMENTS
BLOCK_LON = 150
LIST_MAX = 5
TOP = 32000.0
PARTS = ((0, 0, 48), (1, 0, 48))
MESH = pl.DeviceIdType.MESH


def tables():
    points = np.arange(NLON)[:, None]
    numbers = np.arange(KMAX)[None, :]
    radians = (points * numbers % NLON) * (2.0 * math.pi / NLON)
    both = np.concatenate([np.sin(radians), np.cos(radians)], axis=1)
    weights = np.where(np.arange(KMAX) == 0, 1.0, 2.0) / NLON
    forward = both.reshape(SEGMENTS, SEG, COEFS).transpose(0, 2, 1)
    inverse = (both * np.concatenate([weights, weights])).reshape(SEGMENTS, SEG, COEFS)

    def split_table(table):
        high = table.astype(ml_dtypes.bfloat16)
        low = (table - high.astype(np.float64)).astype(ml_dtypes.bfloat16)
        return np.stack([high, low], axis=1)

    return split_table(forward), split_table(inverse)


def split(value):
    high = value.astype(jnp.bfloat16)
    return high, (value - high.astype(jnp.float32)).astype(jnp.bfloat16)


def dot(a, b):
    return jnp.dot(a, b, preferred_element_type=jnp.float32)


def dot3(table, value):
    high, low = split(value)
    return dot(table[0], high) + (dot(table[1], high) + dot(table[0], low))


def encode(value):
    top = jnp.maximum(jnp.max(jnp.abs(value), axis=0, keepdims=True), 1e-30)
    whole = jnp.floor(value * (TOP / top) + 0.5)
    return whole.astype(jnp.int32).astype(jnp.int16), top * (1.0 / TOP)


def decode(code, scale):
    return code.astype(jnp.int32).astype(jnp.float32) * scale


def silu(v):
    return v * (0.5 + 0.5 * jnp.tanh(0.5 * v))


def kernel(
    state, cutoffs, listed, w_in, w_mid, w_out, forward, inverse, out,
    x_v, f_v, i_v, wi_v, wm_v, wo_v, part_v, part_s, got_v, got_s, sum_v, sum_s, all_v, all_s, out_v,
    load_sem, store_sem, s1, r1, s2, r2,
):
    me = lax.axis_index("tiles")
    seat = me // LATS
    lat = lax.rem(me, LATS)
    other = lax.rem(lat + LATS // 2, LATS)
    z = seat // 2
    seats = [lax.rem(z + dz, 4) * 2 + side for dz in (2, 1, 3, 0) for side in (0, 1)]

    barrier = pltpu.get_barrier_semaphore()
    for j in seats:
        pl.semaphore_signal(barrier, inc=1, device_id=(j * LATS + other,), device_id_type=MESH)

    loads = [
        pltpu.make_async_copy(src, dst, load_sem.at[i])
        for i, (src, dst) in enumerate(
            (
                (state.at[0, :, 0, :], x_v.at[0]),
                (forward.at[seat], f_v),
                (state.at[0, :, 1, :], x_v.at[1]),
                (inverse.at[seat], i_v),
                (w_in, wi_v),
                (w_mid, wm_v),
                (w_out, wo_v),
            )
        )
    ]
    for load in loads:
        load.start()

    def pair(part, slot, code, scale, code_to, scale_to, send_sem, recv_sem, j, owner):
        return [
            pltpu.make_async_remote_copy(
                src_ref=src,
                dst_ref=dst,
                send_sem=send_sem.at[what, part, slot],
                recv_sem=recv_sem.at[what, part, owner],
                device_id=(j * LATS + other,),
                device_id_type=MESH,
            )
            for what, (src, dst) in enumerate(((scale, scale_to), (code, code_to)))
        ]

    def coefs(j, first, size):
        return pl.ds(pl.multiple_of(j * OWNED + first, 16), size)

    sent = []
    for row in range(ROWS):
        if row == 0:
            loads[0].wait()
            loads[1].wait()
        else:
            loads[2].wait()
        part_v[row], part_s[row] = encode(dot3(f_v, x_v[row]))
        if row == 0:
            pl.semaphore_wait(barrier, SEGMENTS)
        for part, (at, first, size) in enumerate(PARTS):
            if at == row:
                for slot, j in enumerate(seats):
                    copies = pair(
                        part, slot,
                        part_v.at[row, coefs(j, first, size)], part_s.at[row],
                        got_v.at[seat, row, pl.ds(first, size)], got_s.at[part, seat],
                        s1, r1, j, seat,
                    )
                    for copy in copies:
                        copy.start()
                    sent += copies

    for part, (row, first, size) in enumerate(PARTS):
        total = None
        for j in range(SEGMENTS):
            code, scale = got_v.at[j, row, pl.ds(first, size)], got_s.at[part, j]
            for copy in pair(part, 0, code, scale, code, scale, s1, r1, j, j):
                copy.wait_recv()
            value = decode(code[...], scale[...])
            total = value if total is None else total + value
        number = lax.rem(seat, 4) * OWNED + first + lax.broadcasted_iota(jnp.int32, (size, 1), 0)
        total = jnp.where(number <= cutoffs[other * ROWS + row], total, 0.0)
        sum_v[row, pl.ds(first, size)], sum_s[part] = encode(total)
        for slot, j in enumerate(seats):
            copies = pair(
                part, slot,
                sum_v.at[row, pl.ds(first, size)], sum_s.at[part],
                all_v.at[row, coefs(seat, first, size)], all_s.at[part, seat],
                s2, r2, j, seat,
            )
            for copy in copies:
                copy.start()
            sent += copies

    for i in range(3, 7):
        loads[i].wait()
    point = lax.broadcasted_iota(jnp.int32, (SEG, 1), 0)
    stores = []
    for row in range(ROWS):
        pieces = {}
        for part, (at, first, size) in enumerate(PARTS):
            if at == row:
                for j in range(SEGMENTS):
                    code, scale = all_v.at[row, pl.ds(j * OWNED + first, size)], all_s.at[part, j]
                    for copy in pair(part, 0, code, scale, code, scale, s2, r2, j, j):
                        copy.wait_recv()
                    pieces[j * OWNED + first] = decode(code[...], scale[...])
        smooth = dot3(i_v, jnp.concatenate([pieces[k] for k in sorted(pieces)], axis=0))
        h = smooth.astype(jnp.bfloat16)
        h = silu(dot(h, wi_v[...])).astype(jnp.bfloat16)
        h = silu(dot(h, wm_v[...])).astype(jnp.bfloat16)
        tendency = dot(h, wo_v[...])
        block = 3 * row + jnp.where(point >= BLOCK_LON, 1, 0) + jnp.where(point >= 2 * BLOCK_LON, 1, 0)
        hit = block == listed[0, 0]
        for i in range(1, LIST_MAX):
            hit = jnp.logical_or(hit, block == listed[0, i])
        out_v[row] = smooth + jnp.where(hit, tendency, 0.0)
        store = pltpu.make_async_copy(out_v.at[row], out.at[0, :, row, :], store_sem.at[row])
        store.start()
        stores.append(store)
    for copy in sent:
        copy.wait_send()
    for store in stores:
        store.wait()


def local(forward, inverse, state, cutoffs, listed, w_in, w_mid, w_out):
    hbm = pl.BlockSpec(memory_space=pl.ANY)
    smem = pl.BlockSpec(memory_space=pltpu.SMEM)
    parts = len(PARTS)
    hidden = w_mid.shape[0]
    f32, bf16, i16 = jnp.float32, jnp.bfloat16, jnp.int16
    dma = pltpu.SemaphoreType.DMA
    result = pl.pallas_call(
        kernel,
        out_shape=jax.ShapeDtypeStruct((1, SEG, ROWS, CHANNELS), f32),
        in_specs=[hbm, smem, smem, hbm, hbm, hbm, hbm, hbm],
        out_specs=hbm,
        scratch_shapes=[
            pltpu.VMEM((ROWS, SEG, CHANNELS), f32),
            pltpu.VMEM((2, COEFS, SEG), bf16),
            pltpu.VMEM((2, SEG, COEFS), bf16),
            pltpu.VMEM((CHANNELS, hidden), bf16),
            pltpu.VMEM((hidden, hidden), bf16),
            pltpu.VMEM((hidden, CHANNELS), bf16),
            pltpu.VMEM((ROWS, COEFS, CHANNELS), i16),
            pltpu.VMEM((ROWS, 1, CHANNELS), f32),
            pltpu.VMEM((SEGMENTS, ROWS, OWNED, CHANNELS), i16),
            pltpu.VMEM((parts, SEGMENTS, 1, CHANNELS), f32),
            pltpu.VMEM((ROWS, OWNED, CHANNELS), i16),
            pltpu.VMEM((parts, 1, CHANNELS), f32),
            pltpu.VMEM((ROWS, COEFS, CHANNELS), i16),
            pltpu.VMEM((parts, SEGMENTS, 1, CHANNELS), f32),
            pltpu.VMEM((ROWS, SEG, CHANNELS), f32),
            dma((7,)),
            dma((ROWS,)),
            dma((2, parts, SEGMENTS)),
            dma((2, parts, SEGMENTS)),
            dma((2, parts, SEGMENTS)),
            dma((2, parts, SEGMENTS)),
        ],
        compiler_params=pltpu.CompilerParams(
            collective_id=0, has_side_effects=True, vmem_limit_bytes=48 << 20
        ),
        cost_estimate=pl.CostEstimate(flops=3_000_000_000, bytes_accessed=6_000_000, transcendentals=1_000_000),
    )(state.transpose(0, 3, 1, 2), cutoffs, listed, w_in, w_mid, w_out, forward, inverse)
    return result.transpose(0, 2, 3, 1)


def solution(mesh):
    forward, inverse = tables()

    def whole(prognostic, cutoffs, listed, weight_in, weight_mid, weight_out):
        return local(
            jnp.asarray(forward), jnp.asarray(inverse), prognostic, cutoffs, listed, weight_in, weight_mid, weight_out
        )

    return jax.shard_map(
        whole,
        mesh=mesh,
        in_specs=(P("tiles", None, None, None), P(), P("tiles", None), P(), P(), P()),
        out_specs=P("tiles", None, None, None),
        check_vma=False,
    )
```

time: 569 us -> 33.6 us (0.06)
  other arithmetic: 274 us -> 0 us
  local copies, waits for them, and re-layouts: 142 us -> 6.76 us
  matrix products: 79.8 us -> 0 us
  waiting for transfers between devices: 52.1 us -> 0 us
  Pallas kernels: 0 us -> 26.5 us
  starting transfers between devices: 16 us -> 0 us
    unnamed x1 -> x0, other arithmetic: 268 us -> none
    dot_general x6 -> x0, matrix products: 79.8 us -> none  [the longest x1 20.3 us: local(): jnp.dot(circles, sine, precision=lax.Precision.HIGHEST, preferred_element...]
    unnamed x13, local copies, waits for them, and re-layouts: 73.3 us -> 6.76 us
    reshape x7 -> x0, local copies, waits for them, and re-layouts: 53.8 us -> none  [the longest x2 43.9 us: local(): smooth = smooth.reshape(1, units_piece, devices * segment)]
    all_to_all x2 -> x0, waiting for transfers between devices: 52.1 us -> none  [the longest x1 28.8 us: local(): lax.all_to_all(pieces, 'tiles', split_axis=0, concat_axis=2, tiled=True)]
    pallas_call x0 -> x1, Pallas kernels: none -> 26.5 us  [local(): pl.pallas_call(kernel, out_shape=jax.ShapeDtypeStruct((1, SEG, ROWS, CHAN...]
    all_to_all x2 -> x0, starting transfers between devices: 16 us -> none  [the longest x1 11.1 us: local(): lax.all_to_all(pieces, 'tiles', split_axis=0, concat_axis=2, tiled=True)]
  transfers between devices with their start and end apart: 2 -> 0, of which waited for: 2 -> 0; matrix products, arithmetic and copies ran while one was open for 0% -> 0% of each run, Pallas kernels for 0% -> 0%
where the time goes in v1:
time: 33.6 us; the launch traced here: 33.3 us
  Pallas kernels  26.5 us (79%)
  local copies, waits for them, and re-layouts  6.76 us (20%)
    pallas_call x1, Pallas kernels, local(): pl.pallas_call(kernel, out_shape=jax.ShapeDtypeStruct((1, SEG, ROWS, CHAN...  26.5 us
    unnamed x13, local copies, waits for them, and re-layouts  6.76 us

profile of v1, /device:TPU:0, one launch (start us, length us, event | category | flops | bytes accessed | tf_op | source)
XLA Modules:
  0.0 33.3 jit_solution(3252909567308665264)
XLA Ops:
  0.0 0.0 copy-start
  0.0 1.3 %copy-done = f32[1,2,384,450]{2,1,3,0:T(2,128)S(1)} copy-done((f32[1,2,384,450]{2,1,3,0:T(2,128)S(1)}, f32[1,2,384,450]{2,1,3,0:T(2,128)}, u32[]{:S(2)}) %copy-start) | copy-done | bytes 1382424
  1.3 0.0 copy-start.1
  1.3 1.0 %copy-done.1 = bf16[512,512]{1,0:T(8,128)(2,1)S(1)} copy-done((bf16[512,512]{1,0:T(8,128)(2,1)S(1)}, bf16[512,512]{1,0:T(8,128)(2,1)}, u32[]{:S(2)}) %copy-start.1) | copy-done | bytes 524312
  2.4 0.0 copy-start.2
  2.4 1.0 %copy-done.2 = bf16[384,512]{1,0:T(8,128)(2,1)S(1)} copy-done((bf16[384,512]{1,0:T(8,128)(2,1)S(1)}, bf16[384,512]{1,0:T(8,128)(2,1)}, u32[]{:S(2)}) %copy-start.2) | copy-done | bytes 393240
  3.4 0.0 copy-start.3
  3.4 1.0 %copy-done.3 = bf16[512,384]{1,0:T(8,128)(2,1)S(1)} copy-done((bf16[512,384]{1,0:T(8,128)(2,1)S(1)}, bf16[512,384]{1,0:T(8,128)(2,1)}, u32[]{:S(2)}) %copy-start.3) | copy-done | bytes 393240
  4.4 0.0 copy-start.4
  4.4 0.7 %copy-done.4 = s32[32]{0:T(128)S(1)} copy-done((s32[32]{0:T(128)S(1)}, s32[32]{0:T(128)}, u32[]{:S(2)}) %copy-start.4) | copy-done | bytes 152
  5.0 0.0 copy-start.5
  5.0 0.7 %copy-done.5 = s32[1,5]{1,0:T(1,128)S(1)} copy-done((s32[1,5]{1,0:T(1,128)S(1)}, s32[1,5]{1,0:T(1,128)}, u32[]{:S(2)}) %copy-start.5) | copy-done | bytes 44
  5.7 26.5 %shard_map.82 = f32[1,450,2,384]{3,2,1,0:T(2,128)S(1)} custom-call(f32[1,450,2,384]{3,2,1,0:T(2,128)S(1)} %bitcast.3, s32[32]{0:T(128)S(1)} %copy-done.4, s32[1,5]{1,0:T(1,128)S(1)} %copy-done.5, bf16[384,512]{1,0:T(8,128)(2,1)S(1)} %copy-done.2, bf16[512,512]{1,0:T(8,128)(2,1)S(1)} %copy-done.1, bf16[512,384]{1,0:T(8,128)(2,1)S(1)} %copy-done.3, ...), custom_call_target="tpu_custom_call" | custom-call | flops 3000000000 | bytes 6000000 | tf_op jit(solution)/shard_map/pallas_call | solution.py:206
  32.2 1.1 %copy.10 = f32[1,2,384,450]{2,1,3,0:T(2,128)} copy(f32[1,2,384,450]{2,1,3,0:T(2,128)S(1)} %bitcast.2) | data formatting | bytes 2764800
Async XLA Ops:
  0.0 1.3 %copy-start = (f32[1,2,384,450]{2,1,3,0:T(2,128)S(1)}, f32[1,2,384,450]{2,1,3,0:T(2,128)}, u32[]{:S(2)}) copy-start(f32[1,2,384,450]{2,1,3,0:T(2,128)} %param.8) | copy-start | bytes 4147204
  1.3 1.0 %copy-start.1 = (bf16[512,512]{1,0:T(8,128)(2,1)S(1)}, bf16[512,512]{1,0:T(8,128)(2,1)}, u32[]{:S(2)}) copy-start(bf16[512,512]{1,0:T(8,128)(2,1)} %w_mid.1) | copy-start | bytes 1572868
  2.4 1.0 %copy-start.2 = (bf16[384,512]{1,0:T(8,128)(2,1)S(1)}, bf16[384,512]{1,0:T(8,128)(2,1)}, u32[]{:S(2)}) copy-start(bf16[384,512]{1,0:T(8,128)(2,1)} %w_in.1) | copy-start | bytes 1179652
  3.4 1.0 %copy-start.3 = (bf16[512,384]{1,0:T(8,128)(2,1)S(1)}, bf16[512,384]{1,0:T(8,128)(2,1)}, u32[]{:S(2)}) copy-start(bf16[512,384]{1,0:T(8,128)(2,1)} %w_out.1) | copy-start | bytes 1179652
  4.4 0.7 %copy-start.4 = (s32[32]{0:T(128)S(1)}, s32[32]{0:T(128)}, u32[]{:S(2)}) copy-start(s32[32]{0:T(128)} %cutoffs.1) | copy-start | bytes 388
  5.0 0.7 %copy-start.5 = (s32[1,5]{1,0:T(1,128)S(1)}, s32[1,5]{1,0:T(1,128)}, u32[]{:S(2)}) copy-start(s32[1,5]{1,0:T(1,128)} %listed.1) | copy-start | bytes 64

commit v2 on v1

--- a/solution.py
+++ b/solution.py
@@ -71,8 +71,8 @@
 
 
 def kernel(
-    state, cutoffs, listed, w_in, w_mid, w_out, forward, inverse, out,
-    x_v, f_v, i_v, wi_v, wm_v, wo_v, part_v, part_s, got_v, got_s, sum_v, sum_s, all_v, all_s, out_v,
+    state, cutoffs_h, listed_h, w_in, w_mid, w_out, forward, inverse, out,
+    cutoffs, listed, x_v, f_v, i_v, wi_v, wm_v, wo_v, part_v, part_s, got_v, got_s, sum_v, sum_s, all_v, all_s, out_v,
     load_sem, store_sem, s1, r1, s2, r2,
 ):
     me = lax.axis_index("tiles")
@@ -93,6 +93,8 @@
                 (state.at[0, :, 0, :], x_v.at[0]),
                 (forward.at[seat], f_v),
                 (state.at[0, :, 1, :], x_v.at[1]),
+                (cutoffs_h, cutoffs),
+                (listed_h, listed),
                 (inverse.at[seat], i_v),
                 (w_in, wi_v),
                 (w_mid, wm_v),
@@ -142,6 +144,8 @@
                         copy.start()
                     sent += copies
 
+    loads[3].wait()
+    loads[4].wait()
     for part, (row, first, size) in enumerate(PARTS):
         total = None
         for j in range(SEGMENTS):
@@ -164,7 +168,7 @@
                 copy.start()
             sent += copies
 
-    for i in range(3, 7):
+    for i in range(5, 9):
         loads[i].wait()
     point = lax.broadcasted_iota(jnp.int32, (SEG, 1), 0)
     stores = []
@@ -197,18 +201,19 @@
 
 
 def local(forward, inverse, state, cutoffs, listed, w_in, w_mid, w_out):
-    hbm = pl.BlockSpec(memory_space=pl.ANY)
-    smem = pl.BlockSpec(memory_space=pltpu.SMEM)
+    hbm = pl.BlockSpec(memory_space=pltpu.HBM)
     parts = len(PARTS)
     hidden = w_mid.shape[0]
     f32, bf16, i16 = jnp.float32, jnp.bfloat16, jnp.int16
     dma = pltpu.SemaphoreType.DMA
     result = pl.pallas_call(
         kernel,
-        out_shape=jax.ShapeDtypeStruct((1, SEG, ROWS, CHANNELS), f32),
-        in_specs=[hbm, smem, smem, hbm, hbm, hbm, hbm, hbm],
-        out_specs=hbm,
+        out_shape=pltpu.VMEM((1, SEG, ROWS, CHANNELS), f32),
+        in_specs=[hbm] * 8,
+        out_specs=pl.BlockSpec(memory_space=pl.ANY),
         scratch_shapes=[
+            pltpu.SMEM(cutoffs.shape, jnp.int32),
+            pltpu.SMEM(listed.shape, jnp.int32),
             pltpu.VMEM((ROWS, SEG, CHANNELS), f32),
             pltpu.VMEM((2, COEFS, SEG), bf16),
             pltpu.VMEM((2, SEG, COEFS), bf16),
@@ -224,7 +229,7 @@
             pltpu.VMEM((ROWS, COEFS, CHANNELS), i16),
             pltpu.VMEM((parts, SEGMENTS, 1, CHANNELS), f32),
             pltpu.VMEM((ROWS, SEG, CHANNELS), f32),
-            dma((7,)),
+            dma((9,)),
             dma((ROWS,)),
             dma((2, parts, SEGMENTS)),
             dma((2, parts, SEGMENTS)),
@@ -232,7 +237,7 @@
             dma((2, parts, SEGMENTS)),
         ],
         compiler_params=pltpu.CompilerParams(
-            collective_id=0, has_side_effects=True, vmem_limit_bytes=48 << 20
+            collective_id=0, has_side_effects=True, vmem_limit_bytes=60 << 20
         ),
         cost_estimate=pl.CostEstimate(flops=3_000_000_000, bytes_accessed=6_000_000, transcendentals=1_000_000),
     )(state.transpose(0, 3, 1, 2), cutoffs, listed, w_in, w_mid, w_out, forward, inverse)

time: 33.6 us -> 27 us (0.80)
  local copies, waits for them, and re-layouts: 6.76 us -> 1.08 us
  Pallas kernels: 26.5 us -> 25.8 us
    unnamed x13 -> x1, local copies, waits for them, and re-layouts: 6.76 us -> 1.08 us
    pallas_call x1, Pallas kernels: 26.5 us -> 25.8 us  [local(): pl.pallas_call(kernel, out_shape=pltpu.VMEM((1, SEG, ROWS, CHANNELS), f32...]
where the time goes in v2:
time: 27 us; the launch traced here: 26.9 us
  Pallas kernels  25.8 us (96%)
  local copies, waits for them, and re-layouts  1.08 us (4%)
    pallas_call x1, Pallas kernels, local(): pl.pallas_call(kernel, out_shape=pltpu.VMEM((1, SEG, ROWS, CHANNELS), f32...  25.8 us
    unnamed x1, local copies, waits for them, and re-layouts  1.08 us

profile of v2, /device:TPU:0, one launch (start us, length us, event | category | flops | bytes accessed | tf_op | source)
XLA Modules:
  0.0 26.9 jit_solution(6965219289417663609)
XLA Ops:
  0.0 25.8 %shard_map.82 = f32[1,450,2,384]{3,2,1,0:T(2,128)S(1)} custom-call(f32[1,450,2,384]{3,2,1,0:T(2,128)} %bitcast.3, s32[32]{0:T(128)} %cutoffs_h.1, s32[1,5]{1,0:T(1,128)} %listed_h.1, bf16[384,512]{1,0:T(8,128)(2,1)} %w_in.1, bf16[512,512]{1,0:T(8,128)(2,1)} %w_mid.1, bf16[512,384]{1,0:T(8,128)(2,1)} %w_out.1, ...), custom_call_target="tpu_custom_call" | custom-call | flops 3000000000 | bytes 6000000 | tf_op jit(solution)/shard_map/pallas_call | solution.py:209
  25.8 1.1 %copy.10 = f32[1,2,384,450]{2,1,3,0:T(2,128)} copy(f32[1,2,384,450]{2,1,3,0:T(2,128)S(1)} %bitcast.2) | data formatting | bytes 2764800

commit v3 on v2

--- a/solution.py
+++ b/solution.py
@@ -72,8 +72,8 @@
 
 def kernel(
     state, cutoffs_h, listed_h, w_in, w_mid, w_out, forward, inverse, out,
-    cutoffs, listed, x_v, f_v, i_v, wi_v, wm_v, wo_v, part_v, part_s, got_v, got_s, sum_v, sum_s, all_v, all_s, out_v,
-    load_sem, store_sem, s1, r1, s2, r2,
+    cutoffs, listed, x_v, f_v, i_v, wi_v, wm_v, wo_v, part_v, part_s, got_v, got_s, sum_v, sum_s, all_v, all_s,
+    load_sem, s1, r1, s2, r2,
 ):
     me = lax.axis_index("tiles")
     seat = me // LATS
@@ -171,7 +171,6 @@
     for i in range(5, 9):
         loads[i].wait()
     point = lax.broadcasted_iota(jnp.int32, (SEG, 1), 0)
-    stores = []
     for row in range(ROWS):
         pieces = {}
         for part, (at, first, size) in enumerate(PARTS):
@@ -190,12 +189,15 @@
         hit = block == listed[0, 0]
         for i in range(1, LIST_MAX):
             hit = jnp.logical_or(hit, block == listed[0, i])
-        out_v[row] = smooth + jnp.where(hit, tendency, 0.0)
-        store = pltpu.make_async_copy(out_v.at[row], out.at[0, :, row, :], store_sem.at[row])
-        store.start()
-        stores.append(store)
+        out[row] = smooth + jnp.where(hit, tendency, 0.0)
     for copy in sent:
         copy.wait_send()
+
+
+def place(rows, out, sem):
+    stores = [pltpu.make_async_copy(rows.at[row], out.at[0, :, row, :], sem.at[row]) for row in range(ROWS)]
+    for store in stores:
+        store.start()
     for store in stores:
         store.wait()
 
@@ -208,9 +210,9 @@
     dma = pltpu.SemaphoreType.DMA
     result = pl.pallas_call(
         kernel,
-        out_shape=pltpu.VMEM((1, SEG, ROWS, CHANNELS), f32),
+        out_shape=pltpu.VMEM((ROWS, SEG, CHANNELS), f32),
         in_specs=[hbm] * 8,
-        out_specs=pl.BlockSpec(memory_space=pl.ANY),
+        out_specs=pl.BlockSpec(memory_space=pltpu.VMEM),
         scratch_shapes=[
             pltpu.SMEM(cutoffs.shape, jnp.int32),
             pltpu.SMEM(listed.shape, jnp.int32),
@@ -228,9 +230,7 @@
             pltpu.VMEM((parts, 1, CHANNELS), f32),
             pltpu.VMEM((ROWS, COEFS, CHANNELS), i16),
             pltpu.VMEM((parts, SEGMENTS, 1, CHANNELS), f32),
-            pltpu.VMEM((ROWS, SEG, CHANNELS), f32),
             dma((9,)),
-            dma((ROWS,)),
             dma((2, parts, SEGMENTS)),
             dma((2, parts, SEGMENTS)),
             dma((2, parts, SEGMENTS)),
@@ -241,6 +241,13 @@
         ),
         cost_estimate=pl.CostEstimate(flops=3_000_000_000, bytes_accessed=6_000_000, transcendentals=1_000_000),
     )(state.transpose(0, 3, 1, 2), cutoffs, listed, w_in, w_mid, w_out, forward, inverse)
+    result = pl.pallas_call(
+        place,
+        out_shape=jax.ShapeDtypeStruct((1, SEG, ROWS, CHANNELS), f32),
+        in_specs=[pl.BlockSpec(memory_space=pltpu.VMEM)],
+        out_specs=hbm,
+        scratch_shapes=[dma((ROWS,))],
+    )(pltpu.with_memory_space_constraint(result, pltpu.VMEM))
     return result.transpose(0, 2, 3, 1)
 
 

time: 27 us -> 26.2 us (0.970)
  local copies, waits for them, and re-layouts: 1.08 us -> 0 us
  Pallas kernels: 25.8 us -> 26.1 us
    unnamed x1 -> x0, local copies, waits for them, and re-layouts: 1.08 us -> none
    pallas_call x1 -> x2, Pallas kernels: 25.8 us -> 26.1 us  [the longest x1 25 us: local(): pl.pallas_call(kernel, out_shape=pltpu.VMEM((ROWS, SEG, CHANNELS), f32),...]
where the time goes in v3:
time: 26.2 us; the launch traced here: 26.1 us
  Pallas kernels  26.1 us (100%)
    pallas_call x1, Pallas kernels, local(): pl.pallas_call(kernel, out_shape=pltpu.VMEM((ROWS, SEG, CHANNELS), f32),...  25 us
    pallas_call x1, Pallas kernels, local(): pl.pallas_call(place, out_shape=jax.ShapeDtypeStruct((1, SEG, ROWS, CHANN...  1.1 us

profile of v3, /device:TPU:0, one launch (start us, length us, event | category | flops | bytes accessed | tf_op | source)
XLA Modules:
  0.0 26.1 jit_solution(9534915386187288882)
XLA Ops:
  0.0 25.0 %shard_map.82.rows = f32[2,450,384]{2,1,0:T(8,128)S(1)} custom-call(f32[1,450,2,384]{3,2,1,0:T(2,128)} %bitcast.2, s32[32]{0:T(128)} %cutoffs_h.1, s32[1,5]{1,0:T(1,128)} %listed_h.1, bf16[384,512]{1,0:T(8,128)(2,1)} %w_in.1, bf16[512,512]{1,0:T(8,128)(2,1)} %w_mid.1, bf16[512,384]{1,0:T(8,128)(2,1)} %w_out.1, ...), custom_call_target="tpu_custom_call" | custom-call | flops 3000000000 | bytes 6000000 | tf_op jit(solution)/shard_map/pallas_call | solution.py:211
  25.0 1.1 %shard_map.83 = f32[1,450,2,384]{3,2,1,0:T(2,128)} custom-call(f32[2,450,384]{2,1,0:T(8,128)S(1)} %shard_map.82.rows), custom_call_target="tpu_custom_call" | custom-call | tf_op jit(solution)/shard_map/pallas_call | solution.py:244

commit v4 on v3

--- a/solution.py
+++ b/solution.py
@@ -21,7 +21,6 @@
 BLOCK_LON = 150
 LIST_MAX = 5
 TOP = 32000.0
-PARTS = ((0, 0, 48), (1, 0, 48))
 MESH = pl.DeviceIdType.MESH
 
 
@@ -66,8 +65,8 @@
     return code.astype(jnp.int32).astype(jnp.float32) * scale
 
 
-def silu(v):
-    return v * (0.5 + 0.5 * jnp.tanh(0.5 * v))
+def silu_of_half(u):
+    return u + u * jnp.tanh(u)
 
 
 def kernel(
@@ -80,7 +79,10 @@
     lat = lax.rem(me, LATS)
     other = lax.rem(lat + LATS // 2, LATS)
     z = seat // 2
-    seats = [lax.rem(z + dz, 4) * 2 + side for dz in (2, 1, 3, 0) for side in (0, 1)]
+    seats = [
+        lax.rem(z + dz, 4) * 2 + side
+        for dz, side in ((2, 0), (2, 1), (1, 0), (3, 1), (1, 1), (3, 0), (0, 0), (0, 1))
+    ]
 
     barrier = pltpu.get_barrier_semaphore()
     for j in seats:
@@ -105,23 +107,25 @@
     for load in loads:
         load.start()
 
-    def pair(part, slot, code, scale, code_to, scale_to, send_sem, recv_sem, j, owner):
+    def move(row, code, scale, code_to, scale_to, send_sem, recv_sem, j):
         return [
             pltpu.make_async_remote_copy(
                 src_ref=src,
                 dst_ref=dst,
-                send_sem=send_sem.at[what, part, slot],
-                recv_sem=recv_sem.at[what, part, owner],
+                send_sem=send_sem.at[what, row],
+                recv_sem=recv_sem.at[what, row],
                 device_id=(j * LATS + other,),
                 device_id_type=MESH,
             )
             for what, (src, dst) in enumerate(((scale, scale_to), (code, code_to)))
         ]
 
-    def coefs(j, first, size):
-        return pl.ds(pl.multiple_of(j * OWNED + first, 16), size)
-
-    sent = []
+    def owned(j):
+        return pl.ds(pl.multiple_of(j * OWNED, 16), OWNED)
+
+    def all_copies(row, code, scale, send_sem, recv_sem):
+        return move(row, code, scale, code, scale, send_sem, recv_sem, seats[0])
+
     for row in range(ROWS):
         if row == 0:
             loads[0].wait()
@@ -131,67 +135,55 @@
         part_v[row], part_s[row] = encode(dot3(f_v, x_v[row]))
         if row == 0:
             pl.semaphore_wait(barrier, SEGMENTS)
-        for part, (at, first, size) in enumerate(PARTS):
-            if at == row:
-                for slot, j in enumerate(seats):
-                    copies = pair(
-                        part, slot,
-                        part_v.at[row, coefs(j, first, size)], part_s.at[row],
-                        got_v.at[seat, row, pl.ds(first, size)], got_s.at[part, seat],
-                        s1, r1, j, seat,
-                    )
-                    for copy in copies:
-                        copy.start()
-                    sent += copies
-
-    loads[3].wait()
-    loads[4].wait()
-    for part, (row, first, size) in enumerate(PARTS):
-        total = None
-        for j in range(SEGMENTS):
-            code, scale = got_v.at[j, row, pl.ds(first, size)], got_s.at[part, j]
-            for copy in pair(part, 0, code, scale, code, scale, s1, r1, j, j):
-                copy.wait_recv()
-            value = decode(code[...], scale[...])
-            total = value if total is None else total + value
-        number = lax.rem(seat, 4) * OWNED + first + lax.broadcasted_iota(jnp.int32, (size, 1), 0)
+        for j in seats:
+            for copy in move(
+                row, part_v.at[row, owned(j)], part_s.at[row], got_v.at[row, seat], got_s.at[row, seat], s1, r1, j
+            ):
+                copy.start()
+
+    for i in range(3, 9):
+        loads[i].wait()
+    wi_v[...] = wi_v[...] * jnp.bfloat16(0.5)
+    wm_v[...] = wm_v[...] * jnp.bfloat16(0.5)
+    for row in range(ROWS):
+        for copies in all_copies(row, got_v.at[row], got_s.at[row], s1, r1):
+            copies.wait_recv()
+        total = decode(got_v[row, 0], got_s[row, 0])
+        for j in range(1, SEGMENTS):
+            total = total + decode(got_v[row, j], got_s[row, j])
+        number = lax.rem(seat, 4) * OWNED + lax.broadcasted_iota(jnp.int32, (OWNED, 1), 0)
         total = jnp.where(number <= cutoffs[other * ROWS + row], total, 0.0)
-        sum_v[row, pl.ds(first, size)], sum_s[part] = encode(total)
-        for slot, j in enumerate(seats):
-            copies = pair(
-                part, slot,
-                sum_v.at[row, pl.ds(first, size)], sum_s.at[part],
-                all_v.at[row, coefs(seat, first, size)], all_s.at[part, seat],
-                s2, r2, j, seat,
-            )
-            for copy in copies:
+        sum_v[row], sum_s[row] = encode(total)
+        for j in seats:
+            for copy in move(
+                row, sum_v.at[row], sum_s.at[row], all_v.at[row, owned(seat)], all_s.at[row, seat], s2, r2, j
+            ):
                 copy.start()
-            sent += copies
-
-    for i in range(5, 9):
-        loads[i].wait()
+
     point = lax.broadcasted_iota(jnp.int32, (SEG, 1), 0)
     for row in range(ROWS):
-        pieces = {}
-        for part, (at, first, size) in enumerate(PARTS):
-            if at == row:
-                for j in range(SEGMENTS):
-                    code, scale = all_v.at[row, pl.ds(j * OWNED + first, size)], all_s.at[part, j]
-                    for copy in pair(part, 0, code, scale, code, scale, s2, r2, j, j):
-                        copy.wait_recv()
-                    pieces[j * OWNED + first] = decode(code[...], scale[...])
-        smooth = dot3(i_v, jnp.concatenate([pieces[k] for k in sorted(pieces)], axis=0))
+        if row > 0:
+            for back in range(ROWS):
+                for copies in all_copies(back, part_v.at[back], got_s.at[back], s1, r1):
+                    copies.wait_send()
+                for copies in all_copies(back, all_v.at[back], all_s.at[back], s2, r2):
+                    copies.wait_send()
+        for copies in all_copies(row, all_v.at[row], all_s.at[row], s2, r2):
+            copies.wait_recv()
+        coefs = jnp.concatenate(
+            [decode(all_v[row, pl.ds(j * OWNED, OWNED)], all_s[row, j]) for j in range(SEGMENTS)], axis=0
+        )
+        high, low = split(coefs)
+        smooth = dot(i_v[0], high) + (dot(i_v[1], high) + dot(i_v[0], low))
         h = smooth.astype(jnp.bfloat16)
-        h = silu(dot(h, wi_v[...])).astype(jnp.bfloat16)
-        h = silu(dot(h, wm_v[...])).astype(jnp.bfloat16)
+        h = silu_of_half(dot(h, wi_v[...])).astype(jnp.bfloat16)
+        h = silu_of_half(dot(h, wm_v[...])).astype(jnp.bfloat16)
         tendency = dot(h, wo_v[...])
         block = 3 * row + jnp.where(point >= BLOCK_LON, 1, 0) + jnp.where(point >= 2 * BLOCK_LON, 1, 0)
         hit = block == listed[0, 0]
         for i in range(1, LIST_MAX):
             hit = jnp.logical_or(hit, block == listed[0, i])
         out[row] = smooth + jnp.where(hit, tendency, 0.0)
-    for copy in sent:
-        copy.wait_send()
 
 
 def place(rows, out, sem):
@@ -204,7 +196,6 @@
 
 def local(forward, inverse, state, cutoffs, listed, w_in, w_mid, w_out):
     hbm = pl.BlockSpec(memory_space=pltpu.HBM)
-    parts = len(PARTS)
     hidden = w_mid.shape[0]
     f32, bf16, i16 = jnp.float32, jnp.bfloat16, jnp.int16
     dma = pltpu.SemaphoreType.DMA
@@ -224,17 +215,17 @@
             pltpu.VMEM((hidden, CHANNELS), bf16),
             pltpu.VMEM((ROWS, COEFS, CHANNELS), i16),
             pltpu.VMEM((ROWS, 1, CHANNELS), f32),
-            pltpu.VMEM((SEGMENTS, ROWS, OWNED, CHANNELS), i16),
-            pltpu.VMEM((parts, SEGMENTS, 1, CHANNELS), f32),
+            pltpu.VMEM((ROWS, SEGMENTS, OWNED, CHANNELS), i16),
+            pltpu.VMEM((ROWS, SEGMENTS, 1, CHANNELS), f32),
             pltpu.VMEM((ROWS, OWNED, CHANNELS), i16),
-            pltpu.VMEM((parts, 1, CHANNELS), f32),
+            pltpu.VMEM((ROWS, 1, CHANNELS), f32),
             pltpu.VMEM((ROWS, COEFS, CHANNELS), i16),
-            pltpu.VMEM((parts, SEGMENTS, 1, CHANNELS), f32),
+            pltpu.VMEM((ROWS, SEGMENTS, 1, CHANNELS), f32),
             dma((9,)),
-            dma((2, parts, SEGMENTS)),
-            dma((2, parts, SEGMENTS)),
-            dma((2, parts, SEGMENTS)),
-            dma((2, parts, SEGMENTS)),
+            dma((2, ROWS)),
+            dma((2, ROWS)),
+            dma((2, ROWS)),
+            dma((2, ROWS)),
         ],
         compiler_params=pltpu.CompilerParams(
             collective_id=0, has_side_effects=True, vmem_limit_bytes=60 << 20

time: 26.2 us -> 24.9 us (0.950)
  Pallas kernels: 26.1 us -> 24.8 us
    pallas_call x1, Pallas kernels: 25 us -> 23.7 us  [local(): pl.pallas_call(kernel, out_shape=pltpu.VMEM((ROWS, SEG, CHANNELS), f32),...]
where the time goes in v4:
time: 24.9 us; the launch traced here: 24.8 us
  Pallas kernels  24.8 us (100%)
    pallas_call x1, Pallas kernels, local(): pl.pallas_call(kernel, out_shape=pltpu.VMEM((ROWS, SEG, CHANNELS), f32),...  23.7 us
    pallas_call x1, Pallas kernels, local(): pl.pallas_call(place, out_shape=jax.ShapeDtypeStruct((1, SEG, ROWS, CHANN...  1.1 us

profile of v4, /device:TPU:0, one launch (start us, length us, event | category | flops | bytes accessed | tf_op | source)
XLA Modules:
  0.0 24.8 jit_solution(427428246975008654)
XLA Ops:
  0.0 23.7 %shard_map.82.rows = f32[2,450,384]{2,1,0:T(8,128)S(1)} custom-call(f32[1,450,2,384]{3,2,1,0:T(2,128)} %bitcast.2, s32[32]{0:T(128)} %cutoffs_h.1, s32[1,5]{1,0:T(1,128)} %listed_h.1, bf16[384,512]{1,0:T(8,128)(2,1)} %w_in.1, bf16[512,512]{1,0:T(8,128)(2,1)} %w_mid.1, bf16[512,384]{1,0:T(8,128)(2,1)} %w_out.1, ...), custom_call_target="tpu_custom_call" | custom-call | flops 3000000000 | bytes 6000000 | tf_op jit(solution)/shard_map/pallas_call | solution.py:202
  23.7 1.1 %shard_map.83 = f32[1,450,2,384]{3,2,1,0:T(2,128)} custom-call(f32[2,450,384]{2,1,0:T(8,128)S(1)} %shard_map.82.rows), custom_call_target="tpu_custom_call" | custom-call | tf_op jit(solution)/shard_map/pallas_call | solution.py:235

commit v5 on v4

--- a/solution.py
+++ b/solution.py
@@ -38,7 +38,8 @@
         low = (table - high.astype(np.float64)).astype(ml_dtypes.bfloat16)
         return np.stack([high, low], axis=1)
 
-    return split_table(forward), split_table(inverse)
+    high, low = split_table(inverse).swapaxes(0, 1)
+    return split_table(forward), np.concatenate([high, low, high], axis=2)
 
 
 def split(value):
@@ -174,7 +175,7 @@
             [decode(all_v[row, pl.ds(j * OWNED, OWNED)], all_s[row, j]) for j in range(SEGMENTS)], axis=0
         )
         high, low = split(coefs)
-        smooth = dot(i_v[0], high) + (dot(i_v[1], high) + dot(i_v[0], low))
+        smooth = dot(i_v[...], jnp.concatenate([high, high, low], axis=0))
         h = smooth.astype(jnp.bfloat16)
         h = silu_of_half(dot(h, wi_v[...])).astype(jnp.bfloat16)
         h = silu_of_half(dot(h, wm_v[...])).astype(jnp.bfloat16)
@@ -209,7 +210,7 @@
             pltpu.SMEM(listed.shape, jnp.int32),
             pltpu.VMEM((ROWS, SEG, CHANNELS), f32),
             pltpu.VMEM((2, COEFS, SEG), bf16),
-            pltpu.VMEM((2, SEG, COEFS), bf16),
+            pltpu.VMEM((SEG, 3 * COEFS), bf16),
             pltpu.VMEM((CHANNELS, hidden), bf16),
             pltpu.VMEM((hidden, hidden), bf16),
             pltpu.VMEM((hidden, CHANNELS), bf16),

time: 24.9 us -> 24.8 us (level)
  no operation moved by 1% of the time
where the time goes in v5:
time: 24.8 us; the launch traced here: 24.7 us
  Pallas kernels  24.7 us (100%)
    pallas_call x1, Pallas kernels, local(): pl.pallas_call(kernel, out_shape=pltpu.VMEM((ROWS, SEG, CHANNELS), f32),...  23.6 us
    pallas_call x1, Pallas kernels, local(): pl.pallas_call(place, out_shape=jax.ShapeDtypeStruct((1, SEG, ROWS, CHANN...  1.1 us

profile of v5, /device:TPU:0, one launch (start us, length us, event | category | flops | bytes accessed | tf_op | source)
XLA Modules:
  0.0 24.7 jit_solution(1263389167031085697)
XLA Ops:
  0.0 23.6 %shard_map.82.rows = f32[2,450,384]{2,1,0:T(8,128)S(1)} custom-call(f32[1,450,2,384]{3,2,1,0:T(2,128)} %bitcast.2, s32[32]{0:T(128)} %cutoffs_h.1, s32[1,5]{1,0:T(1,128)} %listed_h.1, bf16[384,512]{1,0:T(8,128)(2,1)} %w_in.1, bf16[512,512]{1,0:T(8,128)(2,1)} %w_mid.1, bf16[512,384]{1,0:T(8,128)(2,1)} %w_out.1, ...), custom_call_target="tpu_custom_call" | custom-call | flops 3000000000 | bytes 6000000 | tf_op jit(solution)/shard_map/pallas_call | solution.py:203
  23.6 1.1 %shard_map.83 = f32[1,450,2,384]{3,2,1,0:T(2,128)} custom-call(f32[2,450,384]{2,1,0:T(8,128)S(1)} %shard_map.82.rows), custom_call_target="tpu_custom_call" | custom-call | tf_op jit(solution)/shard_map/pallas_call | solution.py:236

commit v6 on v5

--- a/solution.py
+++ b/solution.py
@@ -70,13 +70,33 @@
     return u + u * jnp.tanh(u)
 
 
+def finish(row, codes, scales, table, w_in, w_mid, w_out, listed, ready=None):
+    coefs = jnp.concatenate([decode(codes[pl.ds(j * OWNED, OWNED)], scales[j]) for j in range(SEGMENTS)], axis=0)
+    high, low = split(coefs)
+    smooth = dot(table[...], jnp.concatenate([high, high, low], axis=0))
+    h = smooth.astype(jnp.bfloat16)
+    h = silu_of_half(dot(h, w_in[...])).astype(jnp.bfloat16)
+    h = silu_of_half(dot(h, w_mid[...])).astype(jnp.bfloat16)
+    tendency = dot(h, w_out[...])
+    if ready is not None:
+        ready()
+    point = lax.broadcasted_iota(jnp.int32, (SEG, 1), 0)
+    block = 3 * row + jnp.where(point >= BLOCK_LON, 1, 0) + jnp.where(point >= 2 * BLOCK_LON, 1, 0)
+    hit = block == listed[0, 0]
+    for i in range(1, LIST_MAX):
+        hit = jnp.logical_or(hit, block == listed[0, i])
+    return smooth + jnp.where(hit, tendency, 0.0)
+
+
 def kernel(
-    state, cutoffs_h, listed_h, w_in, w_mid, w_out, forward, inverse, out,
-    cutoffs, listed, x_v, f_v, i_v, wi_v, wm_v, wo_v, part_v, part_s, got_v, got_s, sum_v, sum_s, all_v, all_s,
+    state, cutoffs_h, listed_h, w_in, w_mid, w_out, forward, inverse,
+    out, code_v, scale_v, i_v, wi_v, wm_v, wo_v,
+    cutoffs, listed, x_v, f_v, part_v, part_s, got_v, got_s, sum_v, sum_s, all_v, all_s,
     load_sem, s1, r1, s2, r2,
 ):
     me = lax.axis_index("tiles")
     seat = me // LATS
+    codes, scales = (all_v, code_v), (all_s, scale_v)
     lat = lax.rem(me, LATS)
     other = lax.rem(lat + LATS // 2, LATS)
     z = seat // 2
@@ -157,42 +177,32 @@
         sum_v[row], sum_s[row] = encode(total)
         for j in seats:
             for copy in move(
-                row, sum_v.at[row], sum_s.at[row], all_v.at[row, owned(seat)], all_s.at[row, seat], s2, r2, j
+                row, sum_v.at[row], sum_s.at[row], codes[row].at[owned(seat)], scales[row].at[seat], s2, r2, j
             ):
                 copy.start()
 
-    point = lax.broadcasted_iota(jnp.int32, (SEG, 1), 0)
+    for copies in all_copies(0, codes[0], scales[0], s2, r2):
+        copies.wait_recv()
+    out[...] = finish(0, codes[0], scales[0], i_v, wi_v, wm_v, wo_v, listed)
     for row in range(ROWS):
-        if row > 0:
-            for back in range(ROWS):
-                for copies in all_copies(back, part_v.at[back], got_s.at[back], s1, r1):
-                    copies.wait_send()
-                for copies in all_copies(back, all_v.at[back], all_s.at[back], s2, r2):
-                    copies.wait_send()
-        for copies in all_copies(row, all_v.at[row], all_s.at[row], s2, r2):
-            copies.wait_recv()
-        coefs = jnp.concatenate(
-            [decode(all_v[row, pl.ds(j * OWNED, OWNED)], all_s[row, j]) for j in range(SEGMENTS)], axis=0
-        )
-        high, low = split(coefs)
-        smooth = dot(i_v[...], jnp.concatenate([high, high, low], axis=0))
-        h = smooth.astype(jnp.bfloat16)
-        h = silu_of_half(dot(h, wi_v[...])).astype(jnp.bfloat16)
-        h = silu_of_half(dot(h, wm_v[...])).astype(jnp.bfloat16)
-        tendency = dot(h, wo_v[...])
-        block = 3 * row + jnp.where(point >= BLOCK_LON, 1, 0) + jnp.where(point >= 2 * BLOCK_LON, 1, 0)
-        hit = block == listed[0, 0]
-        for i in range(1, LIST_MAX):
-            hit = jnp.logical_or(hit, block == listed[0, i])
-        out[row] = smooth + jnp.where(hit, tendency, 0.0)
-
-
-def place(rows, out, sem):
-    stores = [pltpu.make_async_copy(rows.at[row], out.at[0, :, row, :], sem.at[row]) for row in range(ROWS)]
-    for store in stores:
-        store.start()
-    for store in stores:
-        store.wait()
+        for copies in all_copies(row, part_v.at[row], got_s.at[row], s1, r1):
+            copies.wait_send()
+        for copies in all_copies(row, codes[row], scales[row], s2, r2):
+            copies.wait_send()
+    for copies in all_copies(1, codes[1], scales[1], s2, r2):
+        copies.wait_recv()
+
+
+def close(first, code_v, scale_v, i_v, wi_v, wm_v, wo_v, listed_h, out, listed, second, sem):
+    load = pltpu.make_async_copy(listed_h, listed, sem.at[ROWS])
+    load.start()
+    store = pltpu.make_async_copy(first, out.at[0, :, 0, :], sem.at[0])
+    store.start()
+    second[...] = finish(1, code_v, scale_v, i_v, wi_v, wm_v, wo_v, listed, load.wait)
+    last = pltpu.make_async_copy(second, out.at[0, :, 1, :], sem.at[1])
+    last.start()
+    store.wait()
+    last.wait()
 
 
 def local(forward, inverse, state, cutoffs, listed, w_in, w_mid, w_out):
@@ -200,46 +210,52 @@
     hidden = w_mid.shape[0]
     f32, bf16, i16 = jnp.float32, jnp.bfloat16, jnp.int16
     dma = pltpu.SemaphoreType.DMA
-    result = pl.pallas_call(
+    vmem = pl.BlockSpec(memory_space=pltpu.VMEM)
+    operands = (state.transpose(0, 3, 1, 2), cutoffs, listed, w_in, w_mid, w_out, forward, inverse)
+    kept = pl.pallas_call(
         kernel,
-        out_shape=pltpu.VMEM((ROWS, SEG, CHANNELS), f32),
-        in_specs=[hbm] * 8,
-        out_specs=pl.BlockSpec(memory_space=pltpu.VMEM),
+        out_shape=[
+            pltpu.VMEM((SEG, CHANNELS), f32),
+            pltpu.VMEM((COEFS, CHANNELS), i16),
+            pltpu.VMEM((SEGMENTS, 1, CHANNELS), f32),
+            pltpu.VMEM((SEG, 3 * COEFS), bf16),
+            pltpu.VMEM((CHANNELS, hidden), bf16),
+            pltpu.VMEM((hidden, hidden), bf16),
+            pltpu.VMEM((hidden, CHANNELS), bf16),
+        ],
+        in_specs=[hbm] * len(operands),
+        out_specs=[vmem] * 7,
         scratch_shapes=[
             pltpu.SMEM(cutoffs.shape, jnp.int32),
             pltpu.SMEM(listed.shape, jnp.int32),
             pltpu.VMEM((ROWS, SEG, CHANNELS), f32),
             pltpu.VMEM((2, COEFS, SEG), bf16),
-            pltpu.VMEM((SEG, 3 * COEFS), bf16),
-            pltpu.VMEM((CHANNELS, hidden), bf16),
-            pltpu.VMEM((hidden, hidden), bf16),
-            pltpu.VMEM((hidden, CHANNELS), bf16),
             pltpu.VMEM((ROWS, COEFS, CHANNELS), i16),
             pltpu.VMEM((ROWS, 1, CHANNELS), f32),
             pltpu.VMEM((ROWS, SEGMENTS, OWNED, CHANNELS), i16),
             pltpu.VMEM((ROWS, SEGMENTS, 1, CHANNELS), f32),
             pltpu.VMEM((ROWS, OWNED, CHANNELS), i16),
             pltpu.VMEM((ROWS, 1, CHANNELS), f32),
-            pltpu.VMEM((ROWS, COEFS, CHANNELS), i16),
-            pltpu.VMEM((ROWS, SEGMENTS, 1, CHANNELS), f32),
+            pltpu.VMEM((COEFS, CHANNELS), i16),
+            pltpu.VMEM((SEGMENTS, 1, CHANNELS), f32),
             dma((9,)),
             dma((2, ROWS)),
             dma((2, ROWS)),
             dma((2, ROWS)),
             dma((2, ROWS)),
         ],
-        compiler_params=pltpu.CompilerParams(
-            collective_id=0, has_side_effects=True, vmem_limit_bytes=60 << 20
-        ),
-        cost_estimate=pl.CostEstimate(flops=3_000_000_000, bytes_accessed=6_000_000, transcendentals=1_000_000),
-    )(state.transpose(0, 3, 1, 2), cutoffs, listed, w_in, w_mid, w_out, forward, inverse)
+        compiler_params=pltpu.CompilerParams(collective_id=0, has_side_effects=True, vmem_limit_bytes=40 << 20),
+        cost_estimate=pl.CostEstimate(flops=2_000_000_000, bytes_accessed=6_000_000, transcendentals=500_000),
+    )(*[pltpu.with_memory_space_constraint(array, pltpu.HBM) for array in operands])
     result = pl.pallas_call(
-        place,
+        close,
         out_shape=jax.ShapeDtypeStruct((1, SEG, ROWS, CHANNELS), f32),
-        in_specs=[pl.BlockSpec(memory_space=pltpu.VMEM)],
+        in_specs=[vmem] * 7 + [hbm],
         out_specs=hbm,
-        scratch_shapes=[dma((ROWS,))],
-    )(pltpu.with_memory_space_constraint(result, pltpu.VMEM))
+        scratch_shapes=[pltpu.SMEM(listed.shape, jnp.int32), pltpu.VMEM((SEG, CHANNELS), f32), dma((ROWS + 1,))],
+        compiler_params=pltpu.CompilerParams(vmem_limit_bytes=40 << 20),
+        cost_estimate=pl.CostEstimate(flops=1_000_000_000, bytes_accessed=2_000_000, transcendentals=500_000),
+    )(*[pltpu.with_memory_space_constraint(array, pltpu.VMEM) for array in kept], pltpu.with_memory_space_constraint(listed, pltpu.HBM))
     return result.transpose(0, 2, 3, 1)
 
 

time: 24.8 us -> 24.7 us (level)
  no operation moved by 1% of the time
where the time goes in v6:
time: 24.7 us; the launch traced here: 24.6 us
  Pallas kernels  24.6 us (100%)
    pallas_call x1, Pallas kernels, local(): pl.pallas_call(kernel, out_shape=[pltpu.VMEM((SEG, CHANNELS), f32), pltpu...  22 us
    pallas_call x1, Pallas kernels, local(): pl.pallas_call(close, out_shape=jax.ShapeDtypeStruct((1, SEG, ROWS, CHANN...  2.53 us

profile of v6, /device:TPU:0, one launch (start us, length us, event | category | flops | bytes accessed | tf_op | source)
XLA Modules:
  0.0 24.6 jit_solution(16594680930247383021)
XLA Ops:
  0.0 22.0 %shard_map.82 = (f32[450,384]{1,0:T(8,128)S(1)}, s16[384,384]{1,0:T(8,128)(2,1)S(1)}, f32[8,1,384]{2,1,0:T(1,128)S(1)}, bf16[450,1152]{1,0:T(8,128)(2,1)S(1)}, b...) custom-call(f32[1,450,2,384]{3,2,1,0:T(2,128)} %bitcast.2, s32[32]{0:T(128)} %cutoffs_h.1, ...), custom_call_target="tpu_custom_call" | custom-call | flops 2000000000 | bytes 6000000 | tf_op jit(solution)/shard_map/pallas_call | solution.py:215
  22.0 2.5 %shard_map.83 = f32[1,450,2,384]{3,2,1,0:T(2,128)} custom-call(f32[450,384]{1,0:T(8,128)S(1)} %get-tuple-element.12.first, s16[384,384]{1,0:T(8,128)(2,1)S(1)} %get-tuple-element.13.code_v, f32[8,1,384]{2,1,0:T(1,128)S(1)} %get-tuple-element.14.scale_v, bf16[450,1152]{1,0:T(8,128)(2,1)S(1)} %get-tuple-element.15.i_v, ...), custom_call_target="tpu_custom_call" | custom-call | flops 1000000000 | bytes 2000000 | tf_op jit(solution)/shard_map/pallas_call | solution.py:250
